TPU v7x, 32 devices: a whole 2x2x4 slice. The times are simulated.
32 devices in a mesh: row: 8 (over y, x, core), col: 4 (over z).
Axes of the slice: x: 2, y: 2, z: 4, core: 2. Of those that a mesh axis runs over, the one named last changes fastest.
Arguments:
- source: bfloat16 [16384, 64], P(('row', 'col')), may hold values from -5 to 5, as said below
- target: bfloat16 [8192, 64], P(('col', 'row')), may hold values from -2 to 2, as said below
Outputs:
- source_potential: float32 [16384], P('row')
- target_potential: float32 [8192], P('col')
Inputs may be any that keep to these rules, and one draw needn't show every extreme that they name: `source`: feature values. `target`: feature values.
All inputs are finite; a program needn't handle non-finite values.
Results may differ from a plain program's by a relative error of at most 0.0003.
Values may be sent and summed in bfloat16 or wider, within the bound.
A program may use at most 64 MiB of HBM per device.

v0:
```python
import math

import jax
import jax.numpy as jnp
from jax import lax
from jax.sharding import PartitionSpec as P

HALVES = 4


SCALE = 0.5
LOWEST = -1e30


def squares(features):
    wide = features.astype(jnp.float32)
    return jnp.sum(wide * wide, axis=1)


def pair_combine(first, second):
    highest = jnp.maximum(first[0], second[0])
    return (
        highest,
        first[1] * jnp.exp(first[0] - highest) + second[1] * jnp.exp(second[0] - highest),
    )


def block_stats(left_feat, left_norms, right_feat, right_norms, right_pots):
    others = right_feat.shape[0]
    block_rows = math.gcd(others, 512)
    blocks = others // block_rows
    slabs = (
        right_feat.reshape(blocks, block_rows, right_feat.shape[1]),
        right_norms.reshape(blocks, block_rows),
        right_pots.reshape(blocks, block_rows),
    )

    def advance(running, slab):
        pieces, piece_norms, piece_pots = slab
        products = lax.dot_general(
            left_feat, pieces, (((1,), (1,)), ((), ())), preferred_element_type=jnp.float32
        )
        scores = (
            piece_pots[None, :] - (left_norms[:, None] + piece_norms[None, :] - 2.0 * products)
        ) / SCALE
        highest = jnp.max(scores, axis=1)
        summed = jnp.sum(jnp.exp(scores - highest[:, None]), axis=1)
        return (pair_combine(running, (highest, summed)), None)

    starting = (
        jnp.full(left_feat.shape[:1], LOWEST, jnp.float32),
        jnp.zeros(left_feat.shape[:1], jnp.float32),
    )
    result, unused = lax.scan(advance, starting, slabs)
    return result


def across_columns(highest, summed):
    overall = lax.pmax(highest, "col")
    summed = lax.psum(summed * jnp.exp(highest - overall), "col")
    highest = overall
    return (highest, summed)


def across_rows(highest, summed):
    overall = lax.pmax(highest, "row")
    summed = lax.psum(summed * jnp.exp(highest - overall), "row")
    highest = overall
    return (highest, summed)


def potential(highest, summed, others):
    return -SCALE * (highest + jnp.log(summed)) + SCALE * jnp.log(jnp.float32(others))


def local(source, target):
    source_rows = lax.all_gather(source, "col", axis=0, tiled=True)
    source_sq = squares(source_rows)
    row_count = source_rows.shape[0]
    col_count = target.shape[0] * lax.axis_size("row")
    sources_all = row_count * lax.axis_size("row")
    targets_all = col_count * lax.axis_size("col")
    source_pot = jnp.zeros((row_count,), jnp.float32)
    target_pot = jnp.zeros((col_count,), jnp.float32)
    target_rows = lax.all_gather(target, "row", axis=0, tiled=True)
    target_sq = squares(target_rows)
    for half_step in range(HALVES):
        if half_step % 2 == 0:
            highest, summed = block_stats(
                source_rows, source_sq, target_rows, target_sq, target_pot
            )
            highest, summed = across_columns(highest, summed)
            source_pot = potential(highest, summed, targets_all)
        else:
            highest, summed = block_stats(
                target_rows, target_sq, source_rows, source_sq, source_pot
            )
            highest, summed = across_rows(highest, summed)
            target_pot = potential(highest, summed, sources_all)
    return (source_pot, target_pot)


def solution(mesh):
    placed = (P(("row", "col"), None), P(("col", "row"), None))
    return jax.shard_map(
        local, mesh=mesh, in_specs=placed, out_specs=(P("row"), P("col")), check_vma=False
    )
```

profile of v0, /device:TPU:0, one launch (start us, length us, event | category | flops | bytes accessed | tf_op | source)
XLA Modules:
  0.0 148.5 jit_solution(8070674276749227873)
XLA Ops:
  0.6 0.9 copy.5
  1.5 11.3 %all_gather.7 = bf16[2048,64]{1,0:T(8,128)(2,1)S(1)} all-gather(bf16[256,64]{1,0:T(8,128)(2,1)S(1)} %copy.5), channel_id=1, replica_groups=mesh['row'=8,'col'=4] {'row'}, dimensions={0}, use_global_device_ids=true | all-gather | bytes 294912 | tf_op jit(solution)/shard_map/all_gather | solution.py:85
  12.8 0.3 multiply_reduce_fusion
  13.2 1.0 copy.4
  14.1 16.4 %all_gather.6 = bf16[2048,64]{1,0:T(8,128)(2,1)S(1)} all-gather(bf16[512,64]{1,0:T(8,128)(2,1)S(1)} %copy.4), channel_id=1, replica_groups=mesh['row'=8,'col'=4] {'col'}, dimensions={0}, use_global_device_ids=true | all-gather | bytes 327680 | tf_op jit(solution)/shard_map/all_gather | solution.py:77
  30.5 0.3 multiply_reduce_fusion.1
  30.9 6.9 %while.52 = (s32[]{:T(128)}, f32[2048]{0:T(1024)S(1)}, f32[2048]{0:T(1024)S(1)}, f32[2048]{0:T(1024)S(1)}, f32[4,512]{1,0:T(4,128)S(1)}, /*index=5*/bf16[4,512,6...) while((s32[]{:T(128)}, f32[2048]{0:T(1024)S(1)}, f32[2048]{0:T(1024)S(1)}, ...), condition=%wide.region_5.6_spmd.clone, body=%wide.region_2.5_spmd.clone.sunk | while | flops 142618624 | bytes 9132143 | solution.py:54
  30.9 1.0 fusion.45
  31.9 0.6 exponential_reduce_fusion.8
  32.6 1.0 fusion.45
  33.7 0.6 exponential_reduce_fusion.8
  34.4 1.0 fusion.45
  35.4 0.6 exponential_reduce_fusion.8
  36.1 1.0 fusion.45
  37.1 0.6 exponential_reduce_fusion.8
  37.8 12.2 %pmax.28 = f32[2048]{0:T(1024)S(1)} all-reduce(f32[2048]{0:T(1024)S(1)} %get-tuple-element.169), channel_id=1, replica_groups=mesh['row'=8,'col'=4] {'col'}, use_global_device_ids=true, to_apply=%region_6.7 | all-reduce | flops 2048 | bytes 16384 | tf_op jit(solution)/shard_map/pmax | solution.py:59
  50.1 8.5 %psum.28 = f32[2048]{0:T(1024)S(1)} all-reduce(f32[2048]{0:T(1024)S(1)} %exponential_multiply_fusion.3), channel_id=1, replica_groups=mesh['row'=8,'col'=4] {'col'}, use_global_device_ids=true, to_apply=%region_7.8 | all-reduce | flops 2048 | bytes 16384 | tf_op jit(solution)/shard_map/psum | solution.py:60
  58.7 7.0 %while.53 = (s32[]{:T(128)}, f32[2048]{0:T(1024)S(1)}, f32[2048]{0:T(1024)S(1)}, f32[4,512]{1,0:T(4,128)S(1)}, f32[2048]{0:T(1024)S(1)}, /*index=5*/f32[4,512]{1...) while((s32[]{:T(128)}, f32[2048]{0:T(1024)S(1)}, ...), condition=%wide.region_11.12_spmd.clone, body=%wide.region_8.11_spmd.clone.sunk | while | flops 142618624 | bytes 9138295 | solution.py:54
  58.7 1.1 fusion.48
  59.8 0.6 exponential_reduce_fusion.9
  60.5 1.1 fusion.48
  61.5 0.6 exponential_reduce_fusion.9
  62.2 1.1 fusion.48
  63.3 0.6 exponential_reduce_fusion.9
  64.0 1.1 fusion.48
  65.0 0.6 exponential_reduce_fusion.9
  65.7 12.1 %pmax.29 = f32[2048]{0:T(1024)S(1)} all-reduce(f32[2048]{0:T(1024)S(1)} %get-tuple-element.171), channel_id=1, replica_groups=mesh['row'=8,'col'=4] {'row'}, use_global_device_ids=true, to_apply=%region_12.13 | all-reduce | flops 2048 | bytes 16384 | tf_op jit(solution)/shard_map/pmax | solution.py:66
  77.9 12.0 %psum.29 = f32[2048]{0:T(1024)S(1)} all-reduce(f32[2048]{0:T(1024)S(1)} %exponential_multiply_fusion.2), channel_id=1, replica_groups=mesh['row'=8,'col'=4] {'row'}, use_global_device_ids=true, to_apply=%region_13.14 | all-reduce | flops 2048 | bytes 16384 | tf_op jit(solution)/shard_map/psum | solution.py:67
  90.0 7.0 %while.54 = (s32[]{:T(128)}, f32[2048]{0:T(1024)S(1)}, f32[2048]{0:T(1024)S(1)}, f32[4,512]{1,0:T(4,128)S(1)}, f32[2048]{0:T(1024)S(1)}, /*index=5*/f32[4,512]{1...) while((s32[]{:T(128)}, f32[2048]{0:T(1024)S(1)}, ...), condition=%wide.region_17.18_spmd.clone, body=%wide.region_14.17_spmd.clone.sunk | while | flops 142618624 | bytes 9138295 | solution.py:54
  90.0 1.0 fusion.51
  91.0 0.6 exponential_reduce_fusion.10
  91.7 1.0 fusion.51
  92.8 0.6 exponential_reduce_fusion.10
  93.5 1.0 fusion.51
  94.5 0.6 exponential_reduce_fusion.10
  95.2 1.0 fusion.51
  96.3 0.6 exponential_reduce_fusion.10
  97.0 10.6 %pmax.30 = f32[2048]{0:T(1024)S(1)} all-reduce(f32[2048]{0:T(1024)S(1)} %get-tuple-element.173), channel_id=1, replica_groups=mesh['row'=8,'col'=4] {'col'}, use_global_device_ids=true, to_apply=%region_18.19 | all-reduce | flops 2048 | bytes 16384 | tf_op jit(solution)/shard_map/pmax | solution.py:59
  107.6 8.5 %psum.30 = f32[2048]{0:T(1024)S(1)} all-reduce(f32[2048]{0:T(1024)S(1)} %exponential_multiply_fusion.1), channel_id=1, replica_groups=mesh['row'=8,'col'=4] {'col'}, use_global_device_ids=true, to_apply=%region_19.20 | all-reduce | flops 2048 | bytes 16384 | tf_op jit(solution)/shard_map/psum | solution.py:60
  116.1 0.0 copy-start
  116.2 0.6 copy-done
  116.7 7.0 %while.55 = (s32[]{:T(128)}, f32[2048]{0:T(1024)S(1)}, f32[2048]{0:T(1024)S(1)}, f32[4,512]{1,0:T(4,128)S(1)}, f32[2048]{0:T(1024)S(1)}, /*index=5*/f32[4,512]{1...) while((s32[]{:T(128)}, f32[2048]{0:T(1024)S(1)}, ...), condition=%wide.region_23.24_spmd.clone, body=%wide.region_20.23_spmd.clone.sunk | while | flops 142618624 | bytes 9138295 | solution.py:54
  116.8 1.1 fusion.54
  117.8 0.6 exponential_reduce_fusion.11
  118.5 1.1 fusion.54
  119.6 0.6 exponential_reduce_fusion.11
  120.3 1.1 fusion.54
  121.3 0.6 exponential_reduce_fusion.11
  122.0 1.1 fusion.54
  123.1 0.6 exponential_reduce_fusion.11
  123.8 12.0 %pmax.31 = f32[2048]{0:T(1024)S(1)} all-reduce(f32[2048]{0:T(1024)S(1)} %get-tuple-element.175), channel_id=1, replica_groups=mesh['row'=8,'col'=4] {'row'}, use_global_device_ids=true, to_apply=%region_24.25 | all-reduce | flops 2048 | bytes 16384 | tf_op jit(solution)/shard_map/pmax | solution.py:66
  135.8 12.0 %psum.31 = f32[2048]{0:T(1024)S(1)} all-reduce(f32[2048]{0:T(1024)S(1)} %exponential_multiply_fusion), channel_id=1, replica_groups=mesh['row'=8,'col'=4] {'row'}, use_global_device_ids=true, to_apply=%region_25.26 | all-reduce | flops 2048 | bytes 16384 | tf_op jit(solution)/shard_map/psum | solution.py:67
  147.9 0.6 multiply_add_fusion
  (52 shorter events, 0.5 us)
Async XLA Ops:
  116.1 0.6 copy-start
where the time goes:
time: 149 us; the launch traced here: 148 us
  blocking collectives  116 us (78%)
  matrix products  16.7 us (11%)
  other arithmetic  11.9 us (8%)
  local copies, waits for them, and re-layouts  2.58 us (2%)
    pmax x2, blocking collectives, across_rows(): overall = lax.pmax(highest, 'row')  24.2 us
    psum x2, blocking collectives, across_rows(): summed = lax.psum(summed * jnp.exp(highest - overall), 'row')  24.1 us
    pmax x2, blocking collectives, across_columns(): overall = lax.pmax(highest, 'col')  22.9 us
    psum x2, blocking collectives, across_columns(): summed = lax.psum(summed * jnp.exp(highest - overall), 'col')  17 us
    dot_general x16, matrix products, advance(): lax.dot_general(left_feat, pieces, (((1,), (1,)), ((), ())), preferred_el...  16.7 us
    all_gather x1, blocking collectives, local(): source_rows = lax.all_gather(source, 'col', axis=0, tiled=True)  16.4 us
    all_gather x1, blocking collectives, local(): target_rows = lax.all_gather(target, 'row', axis=0, tiled=True)  11.3 us
    reduce_sum x16, other arithmetic, advance(): summed = jnp.sum(jnp.exp(scores - highest[:, None]), axis=1)  10.3 us

commit v1 on v0

v1 whole, which is shorter than its diff:
```python
import functools
import math

import jax
import jax.numpy as jnp
from jax import lax
from jax.experimental import pallas as pl
from jax.experimental.pallas import tpu as pltpu
from jax.sharding import PartitionSpec as P

MESH = pl.DeviceIdType.MESH
CHUNK = 128
LANES = 128
NT_DIMS = (((1,), (1,)), ((), ()))


def spread(row):
    return jnp.broadcast_to(row, (CHUNK, LANES)).T


def exact_pieces(squared):
    high = squared.astype(jnp.bfloat16)
    low = (squared - high.astype(jnp.float32)).astype(jnp.bfloat16)
    return high, low


def kernel(
    row_n, col_n, src_ref, tgt_ref, spot_ref, tpot_ref,
    src_all, tgt_all, left, right, squares, block, peaks, sums, scales, column_acc, lse, source_norm, tpot_one,
    first_out, first_in, second_out, second_in, third_out, third_in, fourth_out, fourth_in,
    src_send, src_recv, tgt_send, tgt_recv, x1_send, x1_recv, x2_send, x2_recv, x3_send, x3_recv, x4_send, x4_recv,
):
    my_row, my_col = lax.axis_index("row"), lax.axis_index("col")
    src_piece, depth = src_ref.shape
    tgt_piece = tgt_ref.shape[0]
    rows, cols = src_piece * col_n, tgt_piece * row_n
    chunks, tiles = rows // CHUNK, cols // LANES
    sources_all, targets_all = rows * row_n, cols * col_n
    log_sources, log_targets = math.log(sources_all), math.log(targets_all)

    def col_peer(step):
        return (my_row, lax.rem(my_col + step, col_n))

    def row_peer(step):
        return (lax.rem(my_row + step, row_n), my_col)

    barrier = pltpu.get_barrier_semaphore()
    for step in range(1, row_n):
        pl.semaphore_signal(barrier, inc=1, device_id=row_peer(step), device_id_type=MESH)
    for step in range(1, col_n):
        pl.semaphore_signal(barrier, inc=1, device_id=col_peer(step), device_id_type=MESH)
    pl.semaphore_wait(barrier, row_n + col_n - 2)

    def broadcast(source, landing, slot, send, recv, count, peer):
        copies = []
        for step in range(1, count):
            copy = pltpu.make_async_remote_copy(
                src_ref=source,
                dst_ref=landing.at[slot],
                send_sem=send.at[step - 1],
                recv_sem=recv.at[step - 1],
                device_id=peer(step),
                device_id_type=MESH,
            )
            copy.start()
            copies.append(copy)
        return copies

    src_copies = broadcast(src_ref, src_all, my_col, src_send, src_recv, col_n, col_peer)
    tgt_copies = broadcast(tgt_ref, tgt_all, my_row, tgt_send, tgt_recv, row_n, row_peer)
    src_all[my_col] = src_ref[...]
    tgt_all[my_row] = tgt_ref[...]
    for copy in src_copies + tgt_copies:
        copy.wait()

    def build_left(piece, unused):
        wide = src_all[piece].astype(jnp.float32)
        at = pl.ds(pl.multiple_of(piece * src_piece, src_piece), src_piece)
        left[at, 0:LANES] = jnp.concatenate([4.0 * wide, jnp.full_like(wide, -2.0)], axis=1).astype(jnp.bfloat16)
        left[at, LANES : 2 * LANES] = jnp.concatenate(
            [jnp.full_like(wide, -2.0), jnp.zeros_like(wide)], axis=1
        ).astype(jnp.bfloat16)
        high, low = exact_pieces(wide * wide)
        squares[at, :] = jnp.concatenate([high.astype(jnp.float32), low.astype(jnp.float32)], axis=1).astype(
            jnp.bfloat16
        )
        return unused

    lax.fori_loop(0, col_n, build_left, 0)

    def build_right(piece, unused):
        wide = tgt_all[piece].astype(jnp.float32)
        at = pl.ds(pl.multiple_of(piece * tgt_piece, tgt_piece), tgt_piece)
        high, low = exact_pieces(wide * wide)
        right[at, 0:LANES] = jnp.concatenate([wide, high.astype(jnp.float32)], axis=1).astype(jnp.bfloat16)
        right[at, LANES : 2 * LANES] = jnp.concatenate(
            [low.astype(jnp.float32), jnp.zeros_like(wide)], axis=1
        ).astype(jnp.bfloat16)
        return unused

    lax.fori_loop(0, row_n, build_right, 0)

    def chunk_rows(chunk):
        return pl.ds(pl.multiple_of(chunk * CHUNK, CHUNK), CHUNK)

    def lanes(tile):
        return slice(tile * LANES, (tile + 1) * LANES)

    def half_zero(chunk, unused):
        at = chunk_rows(chunk)
        norm = lax.dot_general(
            jnp.ones((8, 2 * depth), jnp.bfloat16), squares[at, :], NT_DIMS, preferred_element_type=jnp.float32
        )
        source_norm[pl.ds(chunk, 1), :] = norm[0:1, :]
        block[at, :] = lax.dot_general(left[at, :], right[...], NT_DIMS, preferred_element_type=jnp.float32)
        top = block[at, lanes(0)]
        for tile in range(1, tiles):
            top = jnp.maximum(top, block[at, lanes(tile)])
        highest = jnp.max(top, axis=1, keepdims=True)
        total = jnp.exp(block[at, lanes(0)] - highest)
        for tile in range(1, tiles):
            total = total + jnp.exp(block[at, lanes(tile)] - highest)
        first_out[0, pl.ds(chunk, 1), :] = jnp.max(top.T, axis=0, keepdims=True)
        first_out[1, pl.ds(chunk, 1), :] = jnp.sum(total.T, axis=0, keepdims=True)
        return unused

    lax.fori_loop(0, chunks, half_zero, 0)
    copies = broadcast(first_out, first_in, my_col, x1_send, x1_recv, col_n, col_peer)
    first_in[my_col] = first_out[...]
    for copy in copies:
        copy.wait()
    overall = first_in[0, 0]
    for other in range(1, col_n):
        overall = jnp.maximum(overall, first_in[other, 0])
    summed = jnp.zeros_like(overall)
    for other in range(col_n):
        summed = summed + first_in[other, 1] * jnp.exp(first_in[other, 0] - overall)
    lse[...] = overall + jnp.log(summed)

    def half_one(chunk, unused):
        at = chunk_rows(chunk)
        shift = spread(lse[pl.ds(chunk, 1), :])
        for tile in range(tiles):
            shifted = block[at, lanes(tile)] - shift
            highest = jnp.max(shifted, axis=0, keepdims=True)
            value = jnp.exp(shifted - highest)
            block[at, lanes(tile)] = value
            peaks[chunk, tile : tile + 1, :] = highest
            sums[chunk, tile : tile + 1, :] = jnp.sum(value, axis=0, keepdims=True)
        return unused

    lax.fori_loop(0, chunks, half_one, 0)
    overall = peaks[0]
    for chunk in range(1, chunks):
        overall = jnp.maximum(overall, peaks[chunk])
    summed = jnp.zeros_like(overall)
    for chunk in range(chunks):
        summed = summed + sums[chunk] * jnp.exp(peaks[chunk] - overall)
    second_out[0] = overall
    second_out[1] = summed
    copies = broadcast(second_out, second_in, my_row, x2_send, x2_recv, row_n, row_peer)
    second_in[my_row] = second_out[...]
    for copy in copies:
        copy.wait()
    overall = second_in[0, 0]
    for other in range(1, row_n):
        overall = jnp.maximum(overall, second_in[other, 0])
    summed = jnp.zeros_like(overall)
    for other in range(row_n):
        summed = summed + second_in[other, 1] * jnp.exp(second_in[other, 0] - overall)
    tpot_one[...] = 0.5 * (log_sources - log_targets) - 0.5 * (overall + jnp.log(summed))
    inverse = float(sources_all) / summed
    for chunk in range(chunks):
        scales[chunk] = jnp.exp(peaks[chunk] - overall) * inverse

    def half_two(chunk, unused):
        at = chunk_rows(chunk)
        total = block[at, lanes(0)] * scales[chunk, 0:1, :]
        for tile in range(1, tiles):
            total = total + block[at, lanes(tile)] * scales[chunk, tile : tile + 1, :]
        third_out[pl.ds(chunk, 1), :] = jnp.sum(total.T, axis=0, keepdims=True)
        return unused

    lax.fori_loop(0, chunks, half_two, 0)
    copies = broadcast(third_out, third_in, my_col, x3_send, x3_recv, col_n, col_peer)
    third_in[my_col] = third_out[...]
    for copy in copies:
        copy.wait()
    summed = third_in[0]
    for other in range(1, col_n):
        summed = summed + third_in[other]
    spot_ref[...] = source_norm[...] + log_targets - 0.5 * (lse[...] + jnp.log(summed))
    lse[...] = float(targets_all) / summed

    column_acc[...] = jnp.zeros_like(column_acc)

    def half_three(chunk, unused):
        at = chunk_rows(chunk)
        weight = spread(lse[pl.ds(chunk, 1), :])
        for tile in range(tiles):
            weighted = (block[at, lanes(tile)] * weight).reshape(CHUNK // 8, 8, LANES)
            column_acc[tile] += jnp.sum(weighted, axis=0) * scales[chunk, tile : tile + 1, :]
        return unused

    lax.fori_loop(0, chunks, half_three, 0)
    fourth_out[...] = jnp.sum(column_acc[...], axis=1)
    copies = broadcast(fourth_out, fourth_in, my_row, x4_send, x4_recv, row_n, row_peer)
    fourth_in[my_row] = fourth_out[...]
    for copy in copies:
        copy.wait()
    summed = fourth_in[0]
    for other in range(1, row_n):
        summed = summed + fourth_in[other]
    tpot_ref[...] = tpot_one[...] + 0.5 * log_sources - 0.5 * jnp.log(summed)


def local(source, target):
    row_n, col_n = lax.axis_size("row"), lax.axis_size("col")
    src_piece, depth = source.shape
    tgt_piece = target.shape[0]
    rows, cols = src_piece * col_n, tgt_piece * row_n
    chunks, tiles = rows // CHUNK, cols // LANES
    f32, bf16 = jnp.float32, jnp.bfloat16
    vmem = pl.BlockSpec(memory_space=pltpu.VMEM)
    row_sems, col_sems = pltpu.SemaphoreType.DMA((row_n - 1,)), pltpu.SemaphoreType.DMA((col_n - 1,))
    spot, tpot = pl.pallas_call(
        functools.partial(kernel, row_n, col_n),
        out_shape=(
            jax.ShapeDtypeStruct((chunks, LANES), f32),
            jax.ShapeDtypeStruct((tiles, LANES), f32),
        ),
        in_specs=[vmem, vmem],
        out_specs=(vmem, vmem),
        scratch_shapes=[
            pltpu.VMEM((col_n, src_piece, depth), bf16),
            pltpu.VMEM((row_n, tgt_piece, depth), bf16),
            pltpu.VMEM((rows, 2 * LANES), bf16),
            pltpu.VMEM((cols, 2 * LANES), bf16),
            pltpu.VMEM((rows, 2 * depth), bf16),
            pltpu.VMEM((rows, cols), f32),
            pltpu.VMEM((chunks, tiles, LANES), f32),
            pltpu.VMEM((chunks, tiles, LANES), f32),
            pltpu.VMEM((chunks, tiles, LANES), f32),
            pltpu.VMEM((tiles, 8, LANES), f32),
            pltpu.VMEM((chunks, LANES), f32),
            pltpu.VMEM((chunks, LANES), f32),
            pltpu.VMEM((tiles, LANES), f32),
            pltpu.VMEM((2, chunks, LANES), f32),
            pltpu.VMEM((col_n, 2, chunks, LANES), f32),
            pltpu.VMEM((2, tiles, LANES), f32),
            pltpu.VMEM((row_n, 2, tiles, LANES), f32),
            pltpu.VMEM((chunks, LANES), f32),
            pltpu.VMEM((col_n, chunks, LANES), f32),
            pltpu.VMEM((tiles, LANES), f32),
            pltpu.VMEM((row_n, tiles, LANES), f32),
            col_sems, col_sems, row_sems, row_sems,
            col_sems, col_sems, row_sems, row_sems,
            col_sems, col_sems, row_sems, row_sems,
        ],
        compiler_params=pltpu.CompilerParams(
            collective_id=0, has_side_effects=True, vmem_limit_bytes=48 * 1024 * 1024
        ),
    )(source, target)
    return spot.reshape(-1), tpot.reshape(-1)


def solution(mesh):
    placed = (P(("row", "col"), None), P(("col", "row"), None))
    return jax.shard_map(
        local, mesh=mesh, in_specs=placed, out_specs=(P("row"), P("col")), check_vma=False
    )
```

time: 149 us -> 59 us (0.40)
  blocking collectives: 116 us -> 0 us
  Pallas kernels: 0 us -> 55.9 us
  matrix products: 16.7 us -> 0 us
  other arithmetic: 11.9 us -> 0 us
    pallas_call x0 -> x1, Pallas kernels: none -> 55.9 us  [local(): pl.pallas_call(functools.partial(kernel, row_n, col_n), out_shape=(jax.Sh...]
    pmax x4 -> x0, blocking collectives: 47 us -> none  [the longest x2 24.2 us: across_rows(): overall = lax.pmax(highest, 'row')]
    psum x4 -> x0, blocking collectives: 41.1 us -> none  [the longest x2 24.1 us: across_rows(): summed = lax.psum(summed * jnp.exp(highest - overall), 'row')]
    all_gather x2 -> x0, blocking collectives: 27.7 us -> none  [the longest x1 16.4 us: local(): source_rows = lax.all_gather(source, 'col', axis=0, tiled=True)]
    dot_general x16 -> x0, matrix products: 16.7 us -> none  [advance(): lax.dot_general(left_feat, pieces, (((1,), (1,)), ((), ())), preferred_el...]
    reduce_sum x18 -> x0, other arithmetic: 11 us -> none  [the longest x16 10.3 us: advance(): summed = jnp.sum(jnp.exp(scores - highest[:, None]), axis=1)]
where the time goes in v1:
time: 59 us; the launch traced here: 58.8 us
  Pallas kernels  55.9 us (95%)
  local copies, waits for them, and re-layouts  2.22 us (4%)
  between operations  0.66 us (1%)
    pallas_call x1, Pallas kernels, local(): pl.pallas_call(functools.partial(kernel, row_n, col_n), out_shape=(jax.Sh...  55.9 us
    unnamed x6, local copies, waits for them, and re-layouts  2.22 us

profile of v1, /device:TPU:0, one launch (start us, length us, event | category | flops | bytes accessed | tf_op | source)
XLA Modules:
  0.0 58.8 jit_solution(9862048427431716867)
XLA Ops:
  0.6 0.0 copy-start
  0.6 0.9 %copy.5.tgt_ref = bf16[256,64]{1,0:T(8,128)(2,1)S(1)} copy(bf16[256,64]{0,1:T(8,128)(2,1)} %param.3) | data formatting | bytes 65536 | tf_op args[1]
  1.5 0.0 copy-done
  1.6 0.1 copy.4.src_ref
  1.7 55.9 %shard_map.41 = (f32[16,128]{1,0:T(8,128)S(1)}, f32[16,128]{1,0:T(8,128)S(1)}) custom-call(bf16[512,64]{1,0:T(8,128)(2,1)S(1)} %copy.4.src_ref, bf16[256,64]{1,0:T(8,128)(2,1)S(1)} %copy.5.tgt_ref), custom_call_target="tpu_custom_call" | custom-call | tf_op jit(solution)/shard_map/pallas_call | solution.py:226
  57.6 0.6 %copy.8 = f32[2048]{0:T(1024)} copy(f32[2048]{0:T(1024)S(1)} %bitcast.3) | data formatting | bytes 16384
  58.2 0.6 %copy.9 = f32[2048]{0:T(1024)} copy(f32[2048]{0:T(1024)S(1)} %bitcast.2) | data formatting | bytes 16384
Async XLA Ops:
  0.6 0.9 %copy-start = (bf16[512,64]{0,1:T(8,128)(2,1)S(1)}, bf16[512,64]{0,1:T(8,128)(2,1)}, u32[]{:S(2)}) copy-start(bf16[512,64]{0,1:T(8,128)(2,1)} %param.2) | copy-start | bytes 196612

commit v2 on v1

--- a/solution.py
+++ b/solution.py
@@ -11,7 +11,7 @@
 MESH = pl.DeviceIdType.MESH
 CHUNK = 128
 LANES = 128
-NT_DIMS = (((1,), (1,)), ((), ()))
+NN_DIMS = (((1,), (0,)), ((), ()))
 
 
 def spread(row):
@@ -26,13 +26,13 @@
 
 def kernel(
     row_n, col_n, src_ref, tgt_ref, spot_ref, tpot_ref,
-    src_all, tgt_all, left, right, squares, block, peaks, sums, scales, column_acc, lse, source_norm, tpot_one,
+    src_all, tgt_all, left, right, tops, block, peaks, sums, scales, column_acc, lse, source_norm, tpot_one,
     first_out, first_in, second_out, second_in, third_out, third_in, fourth_out, fourth_in,
     src_send, src_recv, tgt_send, tgt_recv, x1_send, x1_recv, x2_send, x2_recv, x3_send, x3_recv, x4_send, x4_recv,
 ):
     my_row, my_col = lax.axis_index("row"), lax.axis_index("col")
-    src_piece, depth = src_ref.shape
-    tgt_piece = tgt_ref.shape[0]
+    depth, src_piece = src_ref.shape
+    tgt_piece = tgt_ref.shape[1]
     rows, cols = src_piece * col_n, tgt_piece * row_n
     chunks, tiles = rows // CHUNK, cols // LANES
     sources_all, targets_all = rows * row_n, cols * col_n
@@ -66,76 +66,128 @@
             copies.append(copy)
         return copies
 
-    src_copies = broadcast(src_ref, src_all, my_col, src_send, src_recv, col_n, col_peer)
+    def send_all(source, target, send, recv, count, peer):
+        copies = []
+        for step in range(1, count):
+            copy = pltpu.make_async_remote_copy(
+                src_ref=source,
+                dst_ref=target,
+                send_sem=send(step - 1),
+                recv_sem=recv,
+                device_id=peer(step),
+                device_id_type=MESH,
+            )
+            copy.start()
+            copies.append(copy)
+        return copies
+
     tgt_copies = broadcast(tgt_ref, tgt_all, my_row, tgt_send, tgt_recv, row_n, row_peer)
+    src_copies = send_all(
+        src_ref, src_all.at[my_col], lambda k: src_send.at[k], src_recv.at[my_col], col_n, col_peer
+    )
     src_all[my_col] = src_ref[...]
     tgt_all[my_row] = tgt_ref[...]
-    for copy in src_copies + tgt_copies:
+    left[:, depth : 3 * depth] = jnp.full((rows, 2 * depth), -2.0, jnp.bfloat16)
+    for copy in tgt_copies:
         copy.wait()
 
-    def build_left(piece, unused):
+    for piece in range(row_n):
+        wide = tgt_all[piece].astype(jnp.float32)
+        high, low = exact_pieces(wide * wide)
+        at = slice(piece * tgt_piece, (piece + 1) * tgt_piece)
+        right[0:depth, at] = tgt_all[piece]
+        right[depth : 2 * depth, at] = high
+        right[2 * depth : 3 * depth, at] = low
+
+    def chunk_rows(chunk):
+        return pl.ds(pl.multiple_of(chunk * CHUNK, CHUNK), CHUNK)
+
+    def lanes(tile):
+        return slice(tile * LANES, (tile + 1) * LANES)
+
+    piece_chunks = src_piece // CHUNK
+    width = math.gcd(cols, 512)
+
+    def half_zero(piece):
         wide = src_all[piece].astype(jnp.float32)
         at = pl.ds(pl.multiple_of(piece * src_piece, src_piece), src_piece)
-        left[at, 0:LANES] = jnp.concatenate([4.0 * wide, jnp.full_like(wide, -2.0)], axis=1).astype(jnp.bfloat16)
-        left[at, LANES : 2 * LANES] = jnp.concatenate(
-            [jnp.full_like(wide, -2.0), jnp.zeros_like(wide)], axis=1
-        ).astype(jnp.bfloat16)
-        high, low = exact_pieces(wide * wide)
-        squares[at, :] = jnp.concatenate([high.astype(jnp.float32), low.astype(jnp.float32)], axis=1).astype(
-            jnp.bfloat16
+        left[at, 0:depth] = (4.0 * wide).T.astype(jnp.bfloat16)
+        norm = jnp.sum(wide * wide, axis=0, keepdims=True)
+        for part in range(piece_chunks):
+            source_norm[pl.ds(piece * piece_chunks + part, 1), :] = norm[:, lanes(part)]
+        top = None
+        for group in range(cols // width):
+            at_cols = slice(group * width, (group + 1) * width)
+            score = lax.dot_general(
+                left[at, :], right[:, at_cols], NN_DIMS, preferred_element_type=jnp.float32
+            )
+            block[at, at_cols] = score
+            for tile in range(width // LANES):
+                part = score[:, lanes(tile)]
+                top = part if top is None else jnp.maximum(top, part)
+        tops[...] = top
+
+        def exponentials(part, unused):
+            at = chunk_rows(piece * piece_chunks + part)
+            top = tops[chunk_rows(part), :]
+            highest = jnp.max(top, axis=1, keepdims=True)
+            total = jnp.exp(block[at, lanes(0)] - highest)
+            for tile in range(1, tiles):
+                total = total + jnp.exp(block[at, lanes(tile)] - highest)
+            first_out[piece, 0, pl.ds(part, 1), :] = jnp.max(top.T, axis=0, keepdims=True)
+            first_out[piece, 1, pl.ds(part, 1), :] = jnp.sum(total.T, axis=0, keepdims=True)
+            return unused
+
+        lax.fori_loop(0, piece_chunks, exponentials, 0)
+        send_all(
+            first_out.at[piece], first_in.at[my_col, piece],
+            lambda k: x1_send.at[k, piece], x1_recv.at[my_col, piece], col_n, col_peer,
         )
-        return unused
-
-    lax.fori_loop(0, col_n, build_left, 0)
-
-    def build_right(piece, unused):
-        wide = tgt_all[piece].astype(jnp.float32)
-        at = pl.ds(pl.multiple_of(piece * tgt_piece, tgt_piece), tgt_piece)
-        high, low = exact_pieces(wide * wide)
-        right[at, 0:LANES] = jnp.concatenate([wide, high.astype(jnp.float32)], axis=1).astype(jnp.bfloat16)
-        right[at, LANES : 2 * LANES] = jnp.concatenate(
-            [low.astype(jnp.float32), jnp.zeros_like(wide)], axis=1
-        ).astype(jnp.bfloat16)
-        return unused
-
-    lax.fori_loop(0, row_n, build_right, 0)
-
-    def chunk_rows(chunk):
-        return pl.ds(pl.multiple_of(chunk * CHUNK, CHUNK), CHUNK)
-
-    def lanes(tile):
-        return slice(tile * LANES, (tile + 1) * LANES)
-
-    def half_zero(chunk, unused):
-        at = chunk_rows(chunk)
-        norm = lax.dot_general(
-            jnp.ones((8, 2 * depth), jnp.bfloat16), squares[at, :], NT_DIMS, preferred_element_type=jnp.float32
+        first_in[my_col, piece] = first_out[piece]
+
+    half_zero(my_col)
+
+    def other_piece(step, unused):
+        piece = step + lax.div(step - my_col + col_n, col_n)
+        pltpu.make_async_remote_copy(
+            src_ref=src_ref,
+            dst_ref=src_all.at[piece],
+            send_sem=src_send.at[0],
+            recv_sem=src_recv.at[piece],
+            device_id=col_peer(1),
+            device_id_type=MESH,
+        ).wait_recv()
+        half_zero(piece)
+        return unused
+
+    lax.fori_loop(0, col_n - 1, other_piece, 0)
+    for copy in src_copies:
+        copy.wait_send()
+
+    def first_copy(step, sender, piece):
+        return pltpu.make_async_remote_copy(
+            src_ref=first_out.at[piece],
+            dst_ref=first_in.at[sender, piece],
+            send_sem=x1_send.at[step - 1, piece],
+            recv_sem=x1_recv.at[sender, piece],
+            device_id=col_peer(step),
+            device_id_type=MESH,
         )
-        source_norm[pl.ds(chunk, 1), :] = norm[0:1, :]
-        block[at, :] = lax.dot_general(left[at, :], right[...], NT_DIMS, preferred_element_type=jnp.float32)
-        top = block[at, lanes(0)]
-        for tile in range(1, tiles):
-            top = jnp.maximum(top, block[at, lanes(tile)])
-        highest = jnp.max(top, axis=1, keepdims=True)
-        total = jnp.exp(block[at, lanes(0)] - highest)
-        for tile in range(1, tiles):
-            total = total + jnp.exp(block[at, lanes(tile)] - highest)
-        first_out[0, pl.ds(chunk, 1), :] = jnp.max(top.T, axis=0, keepdims=True)
-        first_out[1, pl.ds(chunk, 1), :] = jnp.sum(total.T, axis=0, keepdims=True)
-        return unused
-
-    lax.fori_loop(0, chunks, half_zero, 0)
-    copies = broadcast(first_out, first_in, my_col, x1_send, x1_recv, col_n, col_peer)
-    first_in[my_col] = first_out[...]
-    for copy in copies:
-        copy.wait()
-    overall = first_in[0, 0]
-    for other in range(1, col_n):
-        overall = jnp.maximum(overall, first_in[other, 0])
-    summed = jnp.zeros_like(overall)
-    for other in range(col_n):
-        summed = summed + first_in[other, 1] * jnp.exp(first_in[other, 0] - overall)
-    lse[...] = overall + jnp.log(summed)
+
+    def finish_rows(piece, unused):
+        for step in range(1, col_n):
+            first_copy(step, lax.rem(my_col + step, col_n), piece).wait()
+        overall = first_in[0, piece, 0]
+        for other in range(1, col_n):
+            overall = jnp.maximum(overall, first_in[other, piece, 0])
+        summed = jnp.zeros_like(overall)
+        for other in range(col_n):
+            summed = summed + first_in[other, piece, 1] * jnp.exp(first_in[other, piece, 0] - overall)
+        total = overall + jnp.log(summed)
+        for part in range(piece_chunks):
+            lse[pl.ds(piece * piece_chunks + part, 1), :] = total[part : part + 1, :]
+        lax.fori_loop(piece * piece_chunks, (piece + 1) * piece_chunks, half_one, 0)
+        return unused
 
     def half_one(chunk, unused):
         at = chunk_rows(chunk)
@@ -149,7 +201,7 @@
             sums[chunk, tile : tile + 1, :] = jnp.sum(value, axis=0, keepdims=True)
         return unused
 
-    lax.fori_loop(0, chunks, half_one, 0)
+    lax.fori_loop(0, col_n, finish_rows, 0)
     overall = peaks[0]
     for chunk in range(1, chunks):
         overall = jnp.maximum(overall, peaks[chunk])
@@ -232,11 +284,11 @@
         in_specs=[vmem, vmem],
         out_specs=(vmem, vmem),
         scratch_shapes=[
-            pltpu.VMEM((col_n, src_piece, depth), bf16),
-            pltpu.VMEM((row_n, tgt_piece, depth), bf16),
-            pltpu.VMEM((rows, 2 * LANES), bf16),
-            pltpu.VMEM((cols, 2 * LANES), bf16),
-            pltpu.VMEM((rows, 2 * depth), bf16),
+            pltpu.VMEM((col_n, depth, src_piece), bf16),
+            pltpu.VMEM((row_n, depth, tgt_piece), bf16),
+            pltpu.VMEM((rows, 3 * depth), bf16),
+            pltpu.VMEM((3 * depth, cols), bf16),
+            pltpu.VMEM((src_piece, LANES), f32),
             pltpu.VMEM((rows, cols), f32),
             pltpu.VMEM((chunks, tiles, LANES), f32),
             pltpu.VMEM((chunks, tiles, LANES), f32),
@@ -245,22 +297,22 @@
             pltpu.VMEM((chunks, LANES), f32),
             pltpu.VMEM((chunks, LANES), f32),
             pltpu.VMEM((tiles, LANES), f32),
-            pltpu.VMEM((2, chunks, LANES), f32),
-            pltpu.VMEM((col_n, 2, chunks, LANES), f32),
+            pltpu.VMEM((col_n, 2, src_piece // CHUNK, LANES), f32),
+            pltpu.VMEM((col_n, col_n, 2, src_piece // CHUNK, LANES), f32),
             pltpu.VMEM((2, tiles, LANES), f32),
             pltpu.VMEM((row_n, 2, tiles, LANES), f32),
             pltpu.VMEM((chunks, LANES), f32),
             pltpu.VMEM((col_n, chunks, LANES), f32),
             pltpu.VMEM((tiles, LANES), f32),
             pltpu.VMEM((row_n, tiles, LANES), f32),
-            col_sems, col_sems, row_sems, row_sems,
-            col_sems, col_sems, row_sems, row_sems,
+            col_sems, pltpu.SemaphoreType.DMA((col_n,)), row_sems, row_sems,
+            pltpu.SemaphoreType.DMA((col_n - 1, col_n)), pltpu.SemaphoreType.DMA((col_n, col_n)), row_sems, row_sems,
             col_sems, col_sems, row_sems, row_sems,
         ],
         compiler_params=pltpu.CompilerParams(
             collective_id=0, has_side_effects=True, vmem_limit_bytes=48 * 1024 * 1024
         ),
-    )(source, target)
+    )(source.T, target.T)
     return spot.reshape(-1), tpot.reshape(-1)
 
 

time: 59 us -> 43.4 us (0.74)
  Pallas kernels: 55.9 us -> 39.7 us
    pallas_call x1, Pallas kernels: 55.9 us -> 39.7 us  [local(): pl.pallas_call(functools.partial(kernel, row_n, col_n), out_shape=(jax.Sh...]
where the time goes in v2:
time: 43.4 us; the launch traced here: 43.1 us
  Pallas kernels  39.7 us (91%)
  local copies, waits for them, and re-layouts  2.79 us (6%)
  between operations  0.65 us (1%)
    pallas_call x1, Pallas kernels, local(): pl.pallas_call(functools.partial(kernel, row_n, col_n), out_shape=(jax.Sh...  39.7 us
    unnamed x6, local copies, waits for them, and re-layouts  2.79 us

profile of v2, /device:TPU:0, one launch (start us, length us, event | category | flops | bytes accessed | tf_op | source)
XLA Modules:
  0.0 43.1 jit_solution(7268495618433337068)
XLA Ops:
  0.6 0.0 copy-start
  0.6 0.8 %copy-done = bf16[512,64]{0,1:T(8,128)(2,1)S(1)} copy-done((bf16[512,64]{0,1:T(8,128)(2,1)S(1)}, bf16[512,64]{0,1:T(8,128)(2,1)}, u32[]{:S(2)}) %copy-start) | copy-done | bytes 65560
  1.5 0.0 copy-start.1
  1.5 0.8 %copy-done.1 = bf16[256,64]{0,1:T(8,128)(2,1)S(1)} copy-done((bf16[256,64]{0,1:T(8,128)(2,1)S(1)}, bf16[256,64]{0,1:T(8,128)(2,1)}, u32[]{:S(2)}) %copy-start.1) | copy-done | bytes 32792
  2.2 39.7 %shard_map.41 = (f32[16,128]{1,0:T(8,128)S(1)}, f32[16,128]{1,0:T(8,128)S(1)}) custom-call(bf16[64,512]{1,0:T(8,128)(2,1)S(1)} %bitcast.4, bf16[64,256]{1,0:T(8,128)(2,1)S(1)} %bitcast.5), custom_call_target="tpu_custom_call" | custom-call | tf_op jit(solution)/shard_map/pallas_call | solution.py:278
  41.9 0.6 %copy.6 = f32[2048]{0:T(1024)} copy(f32[2048]{0:T(1024)S(1)} %bitcast.7) | data formatting | bytes 16384
  42.5 0.6 %copy.7 = f32[2048]{0:T(1024)} copy(f32[2048]{0:T(1024)S(1)} %bitcast.6) | data formatting | bytes 16384
Async XLA Ops:
  0.6 0.8 %copy-start = (bf16[512,64]{0,1:T(8,128)(2,1)S(1)}, bf16[512,64]{0,1:T(8,128)(2,1)}, u32[]{:S(2)}) copy-start(bf16[512,64]{0,1:T(8,128)(2,1)} %param.2) | copy-start | bytes 196612
  1.5 0.8 %copy-start.1 = (bf16[256,64]{0,1:T(8,128)(2,1)S(1)}, bf16[256,64]{0,1:T(8,128)(2,1)}, u32[]{:S(2)}) copy-start(bf16[256,64]{0,1:T(8,128)(2,1)} %param.3) | copy-start | bytes 98308

commit v3 on v2

--- a/solution.py
+++ b/solution.py
@@ -41,6 +41,17 @@
     def col_peer(step):
         return (my_row, lax.rem(my_col + step, col_n))
 
+    def nearest(step):
+        below, above = my_col, col_n - 1 - my_col
+        low_side = lax.div(above - below + col_n, col_n)
+        reach = low_side * below + (1 - low_side) * above
+        both = lax.div(2 * reach - step + col_n, col_n)
+        around = (step + 1) // 2 * (2 * (step % 2) - 1)
+        return my_col + both * around + (1 - both) * (step - reach) * (2 * low_side - 1)
+
+    def near_peer(step):
+        return (my_row, nearest(step))
+
     def row_peer(step):
         return (lax.rem(my_row + step, row_n), my_col)
 
@@ -49,6 +60,9 @@
         pl.semaphore_signal(barrier, inc=1, device_id=row_peer(step), device_id_type=MESH)
     for step in range(1, col_n):
         pl.semaphore_signal(barrier, inc=1, device_id=col_peer(step), device_id_type=MESH)
+    src_all[my_col] = src_ref[...]
+    tgt_all[my_row] = tgt_ref[...]
+    left[:, depth : 3 * depth] = jnp.full((rows, 2 * depth), -2.0, jnp.bfloat16)
     pl.semaphore_wait(barrier, row_n + col_n - 2)
 
     def broadcast(source, landing, slot, send, recv, count, peer):
@@ -81,13 +95,10 @@
             copies.append(copy)
         return copies
 
+    src_copies = send_all(
+        src_ref, src_all.at[my_col], lambda k: src_send.at[k], src_recv.at[my_col], col_n, near_peer
+    )
     tgt_copies = broadcast(tgt_ref, tgt_all, my_row, tgt_send, tgt_recv, row_n, row_peer)
-    src_copies = send_all(
-        src_ref, src_all.at[my_col], lambda k: src_send.at[k], src_recv.at[my_col], col_n, col_peer
-    )
-    src_all[my_col] = src_ref[...]
-    tgt_all[my_row] = tgt_ref[...]
-    left[:, depth : 3 * depth] = jnp.full((rows, 2 * depth), -2.0, jnp.bfloat16)
     for copy in tgt_copies:
         copy.wait()
 
@@ -134,8 +145,9 @@
             total = jnp.exp(block[at, lanes(0)] - highest)
             for tile in range(1, tiles):
                 total = total + jnp.exp(block[at, lanes(tile)] - highest)
-            first_out[piece, 0, pl.ds(part, 1), :] = jnp.max(top.T, axis=0, keepdims=True)
-            first_out[piece, 1, pl.ds(part, 1), :] = jnp.sum(total.T, axis=0, keepdims=True)
+            first_out[piece, pl.ds(part, 1), :] = jnp.max(top.T, axis=0, keepdims=True) + jnp.log(
+                jnp.sum(total.T, axis=0, keepdims=True)
+            )
             return unused
 
         lax.fori_loop(0, piece_chunks, exponentials, 0)
@@ -148,7 +160,7 @@
     half_zero(my_col)
 
     def other_piece(step, unused):
-        piece = step + lax.div(step - my_col + col_n, col_n)
+        piece = nearest(step)
         pltpu.make_async_remote_copy(
             src_ref=src_ref,
             dst_ref=src_all.at[piece],
@@ -160,7 +172,7 @@
         half_zero(piece)
         return unused
 
-    lax.fori_loop(0, col_n - 1, other_piece, 0)
+    lax.fori_loop(1, col_n, other_piece, 0)
     for copy in src_copies:
         copy.wait_send()
 
@@ -174,15 +186,16 @@
             device_id_type=MESH,
         )
 
-    def finish_rows(piece, unused):
+    def finish_rows(place, unused):
+        piece = (col_n - 1) // 2 + (place + 1) // 2 * (2 * (place % 2) - 1)
         for step in range(1, col_n):
             first_copy(step, lax.rem(my_col + step, col_n), piece).wait()
-        overall = first_in[0, piece, 0]
+        overall = first_in[0, piece]
         for other in range(1, col_n):
-            overall = jnp.maximum(overall, first_in[other, piece, 0])
+            overall = jnp.maximum(overall, first_in[other, piece])
         summed = jnp.zeros_like(overall)
         for other in range(col_n):
-            summed = summed + first_in[other, piece, 1] * jnp.exp(first_in[other, piece, 0] - overall)
+            summed = summed + jnp.exp(first_in[other, piece] - overall)
         total = overall + jnp.log(summed)
         for part in range(piece_chunks):
             lse[pl.ds(piece * piece_chunks + part, 1), :] = total[part : part + 1, :]
@@ -208,18 +221,17 @@
     summed = jnp.zeros_like(overall)
     for chunk in range(chunks):
         summed = summed + sums[chunk] * jnp.exp(peaks[chunk] - overall)
-    second_out[0] = overall
-    second_out[1] = summed
+    second_out[...] = overall + jnp.log(summed)
     copies = broadcast(second_out, second_in, my_row, x2_send, x2_recv, row_n, row_peer)
     second_in[my_row] = second_out[...]
     for copy in copies:
         copy.wait()
-    overall = second_in[0, 0]
+    overall = second_in[0]
     for other in range(1, row_n):
-        overall = jnp.maximum(overall, second_in[other, 0])
+        overall = jnp.maximum(overall, second_in[other])
     summed = jnp.zeros_like(overall)
     for other in range(row_n):
-        summed = summed + second_in[other, 1] * jnp.exp(second_in[other, 0] - overall)
+        summed = summed + jnp.exp(second_in[other] - overall)
     tpot_one[...] = 0.5 * (log_sources - log_targets) - 0.5 * (overall + jnp.log(summed))
     inverse = float(sources_all) / summed
     for chunk in range(chunks):
@@ -297,10 +309,10 @@
             pltpu.VMEM((chunks, LANES), f32),
             pltpu.VMEM((chunks, LANES), f32),
             pltpu.VMEM((tiles, LANES), f32),
-            pltpu.VMEM((col_n, 2, src_piece // CHUNK, LANES), f32),
-            pltpu.VMEM((col_n, col_n, 2, src_piece // CHUNK, LANES), f32),
-            pltpu.VMEM((2, tiles, LANES), f32),
-            pltpu.VMEM((row_n, 2, tiles, LANES), f32),
+            pltpu.VMEM((col_n, src_piece // CHUNK, LANES), f32),
+            pltpu.VMEM((col_n, col_n, src_piece // CHUNK, LANES), f32),
+            pltpu.VMEM((tiles, LANES), f32),
+            pltpu.VMEM((row_n, tiles, LANES), f32),
             pltpu.VMEM((chunks, LANES), f32),
             pltpu.VMEM((col_n, chunks, LANES), f32),
             pltpu.VMEM((tiles, LANES), f32),

time: 43.4 us -> 43.1 us (level)
  no operation moved by 1% of the time
where the time goes in v3:
time: 43.1 us; the launch traced here: 42.9 us
  Pallas kernels  39.4 us (91%)
  local copies, waits for them, and re-layouts  2.79 us (6%)
  between operations  0.65 us (2%)
    pallas_call x1, Pallas kernels, local(): pl.pallas_call(functools.partial(kernel, row_n, col_n), out_shape=(jax.Sh...  39.4 us
    unnamed x6, local copies, waits for them, and re-layouts  2.79 us

profile of v3, /device:TPU:0, one launch (start us, length us, event | category | flops | bytes accessed | tf_op | source)
XLA Modules:
  0.0 42.9 jit_solution(5587537616528212505)
XLA Ops:
  0.6 0.0 copy-start
  0.6 0.8 %copy-done = bf16[512,64]{0,1:T(8,128)(2,1)S(1)} copy-done((bf16[512,64]{0,1:T(8,128)(2,1)S(1)}, bf16[512,64]{0,1:T(8,128)(2,1)}, u32[]{:S(2)}) %copy-start) | copy-done | bytes 65560
  1.5 0.0 copy-start.1
  1.5 0.8 %copy-done.1 = bf16[256,64]{0,1:T(8,128)(2,1)S(1)} copy-done((bf16[256,64]{0,1:T(8,128)(2,1)S(1)}, bf16[256,64]{0,1:T(8,128)(2,1)}, u32[]{:S(2)}) %copy-start.1) | copy-done | bytes 32792
  2.2 39.4 %shard_map.41 = (f32[16,128]{1,0:T(8,128)S(1)}, f32[16,128]{1,0:T(8,128)S(1)}) custom-call(bf16[64,512]{1,0:T(8,128)(2,1)S(1)} %bitcast.4, bf16[64,256]{1,0:T(8,128)(2,1)S(1)} %bitcast.5), custom_call_target="tpu_custom_call" | custom-call | tf_op jit(solution)/shard_map/pallas_call | solution.py:290
  41.7 0.6 %copy.6 = f32[2048]{0:T(1024)} copy(f32[2048]{0:T(1024)S(1)} %bitcast.7) | data formatting | bytes 16384
  42.3 0.6 %copy.7 = f32[2048]{0:T(1024)} copy(f32[2048]{0:T(1024)S(1)} %bitcast.6) | data formatting | bytes 16384
Async XLA Ops:
  0.6 0.8 %copy-start = (bf16[512,64]{0,1:T(8,128)(2,1)S(1)}, bf16[512,64]{0,1:T(8,128)(2,1)}, u32[]{:S(2)}) copy-start(bf16[512,64]{0,1:T(8,128)(2,1)} %param.2) | copy-start | bytes 196612
  1.5 0.8 %copy-start.1 = (bf16[256,64]{0,1:T(8,128)(2,1)S(1)}, bf16[256,64]{0,1:T(8,128)(2,1)}, u32[]{:S(2)}) copy-start(bf16[256,64]{0,1:T(8,128)(2,1)} %param.3) | copy-start | bytes 98308

commit v4 on v3

--- a/solution.py
+++ b/solution.py
@@ -26,7 +26,7 @@
 
 def kernel(
     row_n, col_n, src_ref, tgt_ref, spot_ref, tpot_ref,
-    src_all, tgt_all, left, right, tops, block, peaks, sums, scales, column_acc, lse, source_norm, tpot_one,
+    src_all, tgt_all, left, right, tops, row_acc, block, peaks, sums, scales, column_acc, lse, source_norm, tpot_one,
     first_out, first_in, second_out, second_in, third_out, third_in, fourth_out, fourth_in,
     src_send, src_recv, tgt_send, tgt_recv, x1_send, x1_recv, x2_send, x2_recv, x3_send, x3_recv, x4_send, x4_recv,
 ):
@@ -175,6 +175,8 @@
     lax.fori_loop(1, col_n, other_piece, 0)
     for copy in src_copies:
         copy.wait_send()
+
+    half_tiles, half_chunks = tiles // 2, chunks // 2
 
     def first_copy(step, sender, piece):
         return pltpu.make_async_remote_copy(
@@ -199,13 +201,13 @@
         total = overall + jnp.log(summed)
         for part in range(piece_chunks):
             lse[pl.ds(piece * piece_chunks + part, 1), :] = total[part : part + 1, :]
-        lax.fori_loop(piece * piece_chunks, (piece + 1) * piece_chunks, half_one, 0)
-        return unused
-
-    def half_one(chunk, unused):
+        lax.fori_loop(piece * piece_chunks, (piece + 1) * piece_chunks, functools.partial(half_one, 0), 0)
+        return unused
+
+    def half_one(group, chunk, unused):
         at = chunk_rows(chunk)
         shift = spread(lse[pl.ds(chunk, 1), :])
-        for tile in range(tiles):
+        for tile in range(group * half_tiles, (group + 1) * half_tiles):
             shifted = block[at, lanes(tile)] - shift
             highest = jnp.max(shifted, axis=0, keepdims=True)
             value = jnp.exp(shifted - highest)
@@ -215,46 +217,90 @@
         return unused
 
     lax.fori_loop(0, col_n, finish_rows, 0)
-    overall = peaks[0]
-    for chunk in range(1, chunks):
-        overall = jnp.maximum(overall, peaks[chunk])
-    summed = jnp.zeros_like(overall)
-    for chunk in range(chunks):
-        summed = summed + sums[chunk] * jnp.exp(peaks[chunk] - overall)
-    second_out[...] = overall + jnp.log(summed)
-    copies = broadcast(second_out, second_in, my_row, x2_send, x2_recv, row_n, row_peer)
-    second_in[my_row] = second_out[...]
-    for copy in copies:
-        copy.wait()
-    overall = second_in[0]
-    for other in range(1, row_n):
-        overall = jnp.maximum(overall, second_in[other])
-    summed = jnp.zeros_like(overall)
-    for other in range(row_n):
-        summed = summed + jnp.exp(second_in[other] - overall)
-    tpot_one[...] = 0.5 * (log_sources - log_targets) - 0.5 * (overall + jnp.log(summed))
-    inverse = float(sources_all) / summed
-    for chunk in range(chunks):
-        scales[chunk] = jnp.exp(peaks[chunk] - overall) * inverse
+    def group_tiles(group):
+        return slice(group * half_tiles, (group + 1) * half_tiles)
+
+    def start_columns(group):
+        at = group_tiles(group)
+        overall = peaks[0, at]
+        for chunk in range(1, chunks):
+            overall = jnp.maximum(overall, peaks[chunk, at])
+        summed = jnp.zeros_like(overall)
+        for chunk in range(chunks):
+            summed = summed + sums[chunk, at] * jnp.exp(peaks[chunk, at] - overall)
+        result = overall + jnp.log(summed)
+        second_out[at, :] = result
+        second_in[my_row, at, :] = result
+        return send_all(
+            second_out.at[at], second_in.at[my_row, at],
+            lambda k: x2_send.at[group, k], x2_recv.at[group, my_row], row_n, row_peer,
+        )
+
+    def wait_from(group, source, landing, send, recv, count, mine, peer, copies):
+        for copy in copies:
+            copy.wait_send()
+        for step in range(1, count):
+            sender = lax.rem(mine + step, count)
+            pltpu.make_async_remote_copy(
+                src_ref=source, dst_ref=landing(sender), send_sem=send.at[group, 0], recv_sem=recv.at[group, sender],
+                device_id=peer(step), device_id_type=MESH,
+            ).wait_recv()
+
+    def finish_columns(group, copies):
+        at = group_tiles(group)
+        wait_from(
+            group, second_out.at[at], lambda sender: second_in.at[sender, at],
+            x2_send, x2_recv, row_n, my_row, row_peer, copies,
+        )
+        overall = second_in[0, at]
+        for other in range(1, row_n):
+            overall = jnp.maximum(overall, second_in[other, at])
+        summed = jnp.zeros_like(overall)
+        for other in range(row_n):
+            summed = summed + jnp.exp(second_in[other, at] - overall)
+        tpot_one[at, :] = 0.5 * (log_sources - log_targets) - 0.5 * (overall + jnp.log(summed))
+        inverse = float(sources_all) / summed
+        for chunk in range(chunks):
+            scales[chunk, at, :] = jnp.exp(peaks[chunk, at] - overall) * inverse
+
+    def partial_row(chunk, group):
+        at = chunk_rows(chunk)
+        total = None
+        for tile in range(group * half_tiles, (group + 1) * half_tiles):
+            term = block[at, lanes(tile)] * scales[chunk, tile : tile + 1, :]
+            total = term if total is None else total + term
+        return total
+
+    def half_two_first(chunk, unused):
+        row_acc[chunk_rows(chunk), :] = partial_row(chunk, 0)
+        return unused
 
     def half_two(chunk, unused):
-        at = chunk_rows(chunk)
-        total = block[at, lanes(0)] * scales[chunk, 0:1, :]
-        for tile in range(1, tiles):
-            total = total + block[at, lanes(tile)] * scales[chunk, tile : tile + 1, :]
+        total = row_acc[chunk_rows(chunk), :] + partial_row(chunk, 1)
         third_out[pl.ds(chunk, 1), :] = jnp.sum(total.T, axis=0, keepdims=True)
         return unused
 
-    lax.fori_loop(0, chunks, half_two, 0)
-    copies = broadcast(third_out, third_in, my_col, x3_send, x3_recv, col_n, col_peer)
-    third_in[my_col] = third_out[...]
-    for copy in copies:
-        copy.wait()
-    summed = third_in[0]
-    for other in range(1, col_n):
-        summed = summed + third_in[other]
-    spot_ref[...] = source_norm[...] + log_targets - 0.5 * (lse[...] + jnp.log(summed))
-    lse[...] = float(targets_all) / summed
+    first_columns = start_columns(0)
+    lax.fori_loop(0, chunks, functools.partial(half_one, 1), 0)
+    second_columns = start_columns(1)
+    finish_columns(0, first_columns)
+    lax.fori_loop(0, chunks, half_two_first, 0)
+    finish_columns(1, second_columns)
+
+    def group_chunks(group):
+        return slice(group * half_chunks, (group + 1) * half_chunks)
+
+    row_copies = []
+    for group in range(2):
+        at = group_chunks(group)
+        lax.fori_loop(group * half_chunks, (group + 1) * half_chunks, half_two, 0)
+        third_in[my_col, at, :] = third_out[at, :]
+        row_copies.append(
+            send_all(
+                third_out.at[at], third_in.at[my_col, at],
+                lambda k, group=group: x3_send.at[group, k], x3_recv.at[group, my_col], col_n, col_peer,
+            )
+        )
 
     column_acc[...] = jnp.zeros_like(column_acc)
 
@@ -266,7 +312,18 @@
             column_acc[tile] += jnp.sum(weighted, axis=0) * scales[chunk, tile : tile + 1, :]
         return unused
 
-    lax.fori_loop(0, chunks, half_three, 0)
+    for group in range(2):
+        at = group_chunks(group)
+        wait_from(
+            group, third_out.at[at], lambda sender, at=at: third_in.at[sender, at],
+            x3_send, x3_recv, col_n, my_col, col_peer, row_copies[group],
+        )
+        summed = third_in[0, at]
+        for other in range(1, col_n):
+            summed = summed + third_in[other, at]
+        spot_ref[at, :] = source_norm[at, :] + log_targets - 0.5 * (lse[at, :] + jnp.log(summed))
+        lse[at, :] = float(targets_all) / summed
+        lax.fori_loop(group * half_chunks, (group + 1) * half_chunks, half_three, 0)
     fourth_out[...] = jnp.sum(column_acc[...], axis=1)
     copies = broadcast(fourth_out, fourth_in, my_row, x4_send, x4_recv, row_n, row_peer)
     fourth_in[my_row] = fourth_out[...]
@@ -301,6 +358,7 @@
             pltpu.VMEM((rows, 3 * depth), bf16),
             pltpu.VMEM((3 * depth, cols), bf16),
             pltpu.VMEM((src_piece, LANES), f32),
+            pltpu.VMEM((rows, LANES), f32),
             pltpu.VMEM((rows, cols), f32),
             pltpu.VMEM((chunks, tiles, LANES), f32),
             pltpu.VMEM((chunks, tiles, LANES), f32),
@@ -318,8 +376,10 @@
             pltpu.VMEM((tiles, LANES), f32),
             pltpu.VMEM((row_n, tiles, LANES), f32),
             col_sems, pltpu.SemaphoreType.DMA((col_n,)), row_sems, row_sems,
-            pltpu.SemaphoreType.DMA((col_n - 1, col_n)), pltpu.SemaphoreType.DMA((col_n, col_n)), row_sems, row_sems,
-            col_sems, col_sems, row_sems, row_sems,
+            pltpu.SemaphoreType.DMA((col_n - 1, col_n)), pltpu.SemaphoreType.DMA((col_n, col_n)),
+            pltpu.SemaphoreType.DMA((2, row_n - 1)), pltpu.SemaphoreType.DMA((2, row_n)),
+            pltpu.SemaphoreType.DMA((2, col_n - 1)), pltpu.SemaphoreType.DMA((2, col_n)),
+            row_sems, row_sems,
         ],
         compiler_params=pltpu.CompilerParams(
             collective_id=0, has_side_effects=True, vmem_limit_bytes=48 * 1024 * 1024

time: 43.1 us -> 43.3 us (level)
  no operation moved by 1% of the time
where the time goes in v4:
time: 43.3 us; the launch traced here: 43.1 us
  Pallas kernels  39.6 us (91%)
  local copies, waits for them, and re-layouts  2.79 us (6%)
  between operations  0.65 us (2%)
    pallas_call x1, Pallas kernels, local(): pl.pallas_call(functools.partial(kernel, row_n, col_n), out_shape=(jax.Sh...  39.6 us
    unnamed x6, local copies, waits for them, and re-layouts  2.79 us

profile of v4, /device:TPU:0, one launch (start us, length us, event | category | flops | bytes accessed | tf_op | source)
XLA Modules:
  0.0 43.1 jit_solution(17091485482282516402)
XLA Ops:
  0.6 0.0 copy-start
  0.6 0.8 %copy-done = bf16[512,64]{0,1:T(8,128)(2,1)S(1)} copy-done((bf16[512,64]{0,1:T(8,128)(2,1)S(1)}, bf16[512,64]{0,1:T(8,128)(2,1)}, u32[]{:S(2)}) %copy-start) | copy-done | bytes 65560
  1.5 0.0 copy-start.1
  1.5 0.8 %copy-done.1 = bf16[256,64]{0,1:T(8,128)(2,1)S(1)} copy-done((bf16[256,64]{0,1:T(8,128)(2,1)S(1)}, bf16[256,64]{0,1:T(8,128)(2,1)}, u32[]{:S(2)}) %copy-start.1) | copy-done | bytes 32792
  2.2 39.6 %shard_map.41 = (f32[16,128]{1,0:T(8,128)S(1)}, f32[16,128]{1,0:T(8,128)S(1)}) custom-call(bf16[64,512]{1,0:T(8,128)(2,1)S(1)} %bitcast.4, bf16[64,256]{1,0:T(8,128)(2,1)S(1)} %bitcast.5), custom_call_target="tpu_custom_call" | custom-call | tf_op jit(solution)/shard_map/pallas_call | solution.py:347
  41.9 0.6 %copy.6 = f32[2048]{0:T(1024)} copy(f32[2048]{0:T(1024)S(1)} %bitcast.7) | data formatting | bytes 16384
  42.5 0.6 %copy.7 = f32[2048]{0:T(1024)} copy(f32[2048]{0:T(1024)S(1)} %bitcast.6) | data formatting | bytes 16384
Async XLA Ops:
  0.6 0.8 %copy-start = (bf16[512,64]{0,1:T(8,128)(2,1)S(1)}, bf16[512,64]{0,1:T(8,128)(2,1)}, u32[]{:S(2)}) copy-start(bf16[512,64]{0,1:T(8,128)(2,1)} %param.2) | copy-start | bytes 196612
  1.5 0.8 %copy-start.1 = (bf16[256,64]{0,1:T(8,128)(2,1)S(1)}, bf16[256,64]{0,1:T(8,128)(2,1)}, u32[]{:S(2)}) copy-start(bf16[256,64]{0,1:T(8,128)(2,1)} %param.3) | copy-start | bytes 98308

commit v5 on v3

--- a/solution.py
+++ b/solution.py
@@ -80,9 +80,9 @@
             copies.append(copy)
         return copies
 
-    def send_all(source, target, send, recv, count, peer):
+    def send_all(source, target, send, recv, count, peer, first=1):
         copies = []
-        for step in range(1, count):
+        for step in range(first, count):
             copy = pltpu.make_async_remote_copy(
                 src_ref=source,
                 dst_ref=target,
@@ -95,12 +95,16 @@
             copies.append(copy)
         return copies
 
+    near_n = col_n // 2 + 1
     src_copies = send_all(
-        src_ref, src_all.at[my_col], lambda k: src_send.at[k], src_recv.at[my_col], col_n, near_peer
+        src_ref, src_all.at[my_col], lambda k: src_send.at[k], src_recv.at[my_col], near_n, near_peer
     )
     tgt_copies = broadcast(tgt_ref, tgt_all, my_row, tgt_send, tgt_recv, row_n, row_peer)
     for copy in tgt_copies:
         copy.wait()
+    src_copies += send_all(
+        src_ref, src_all.at[my_col], lambda k: src_send.at[k], src_recv.at[my_col], col_n, near_peer, near_n
+    )
 
     for piece in range(row_n):
         wide = tgt_all[piece].astype(jnp.float32)

time: 43.1 us -> 44.1 us (1.023)
  Pallas kernels: 39.4 us -> 40.4 us
    pallas_call x1, Pallas kernels: 39.4 us -> 40.4 us  [local(): pl.pallas_call(functools.partial(kernel, row_n, col_n), out_shape=(jax.Sh...]
where the time goes in v5:
time: 44.1 us; the launch traced here: 43.9 us
  Pallas kernels  40.4 us (92%)
  local copies, waits for them, and re-layouts  2.79 us (6%)
  between operations  0.65 us (1%)
    pallas_call x1, Pallas kernels, local(): pl.pallas_call(functools.partial(kernel, row_n, col_n), out_shape=(jax.Sh...  40.4 us
    unnamed x6, local copies, waits for them, and re-layouts  2.79 us

profile of v5, /device:TPU:0, one launch (start us, length us, event | category | flops | bytes accessed | tf_op | source)
XLA Modules:
  0.0 43.9 jit_solution(4612347532333818810)
XLA Ops:
  0.6 0.0 copy-start
  0.6 0.8 %copy-done = bf16[512,64]{0,1:T(8,128)(2,1)S(1)} copy-done((bf16[512,64]{0,1:T(8,128)(2,1)S(1)}, bf16[512,64]{0,1:T(8,128)(2,1)}, u32[]{:S(2)}) %copy-start) | copy-done | bytes 65560
  1.5 0.0 copy-start.1
  1.5 0.8 %copy-done.1 = bf16[256,64]{0,1:T(8,128)(2,1)S(1)} copy-done((bf16[256,64]{0,1:T(8,128)(2,1)S(1)}, bf16[256,64]{0,1:T(8,128)(2,1)}, u32[]{:S(2)}) %copy-start.1) | copy-done | bytes 32792
  2.2 40.4 %shard_map.41 = (f32[16,128]{1,0:T(8,128)S(1)}, f32[16,128]{1,0:T(8,128)S(1)}) custom-call(bf16[64,512]{1,0:T(8,128)(2,1)S(1)} %bitcast.4, bf16[64,256]{1,0:T(8,128)(2,1)S(1)} %bitcast.5), custom_call_target="tpu_custom_call" | custom-call | tf_op jit(solution)/shard_map/pallas_call | solution.py:294
  42.7 0.6 %copy.6 = f32[2048]{0:T(1024)} copy(f32[2048]{0:T(1024)S(1)} %bitcast.7) | data formatting | bytes 16384
  43.3 0.6 %copy.7 = f32[2048]{0:T(1024)} copy(f32[2048]{0:T(1024)S(1)} %bitcast.6) | data formatting | bytes 16384
Async XLA Ops:
  0.6 0.8 %copy-start = (bf16[512,64]{0,1:T(8,128)(2,1)S(1)}, bf16[512,64]{0,1:T(8,128)(2,1)}, u32[]{:S(2)}) copy-start(bf16[512,64]{0,1:T(8,128)(2,1)} %param.2) | copy-start | bytes 196612
  1.5 0.8 %copy-start.1 = (bf16[256,64]{0,1:T(8,128)(2,1)S(1)}, bf16[256,64]{0,1:T(8,128)(2,1)}, u32[]{:S(2)}) copy-start(bf16[256,64]{0,1:T(8,128)(2,1)} %param.3) | copy-start | bytes 98308
